TPU v7x, 256 devices: a whole 4x4x8 slice. The times are simulated.
256 devices in a mesh: tile: 32 (over x, z_lo, core), lev: 8 (over y, z_hi).
Axes of the slice: x: 4, y: 4, z: 8 (z_hi: 2, z_lo: 4; z = z_hi * 4 + z_lo), core: 2. Of those that a mesh axis runs over, the one named last changes fastest.
Arguments:
- ensemble: bfloat16 [80, 48, 32768], P(None, 'lev', 'tile'), may hold values from -6 to 6
- perturbed: float32 [8, 80, 256], replicated, may hold values from -6 to 6
- factor: float32 [8, 256, 256], replicated, may hold values from -0.04 to 0.32
- obs_tile: int32 [8, 256], replicated, may hold values from 0 to 31, as said below
- obs_column: int32 [8, 256], replicated, may hold values from 0 to 1023
- obs_level: int32 [8, 256], replicated, may hold values from 0 to 47
Outputs:
- posterior: bfloat16 [80, 48, 32768], P(None, 'lev', 'tile')
Inputs may be any that keep to these rules, and one draw needn't show every extreme that they name: `obs_tile`: within each batch the owner tiles never fall; the first observation of a batch lies on tile 0 and the last on tile 32 - 1.
All inputs are finite; a program needn't handle non-finite values.
Results may differ from a plain program's by a relative error of at most 0.0033.
Values sent between devices are 32-bit elements; how exact they have to be, the bound alone decides.
A program may use at most 128 MiB of HBM per device.

v0:
```python
import jax
import jax.numpy as jnp
from jax import lax
from jax.sharding import PartitionSpec as P

MEMBERS = 80
RADIUS = 2560
VREACH = 12


def horizontal(obs_gcol, positions, columns):
    distance = jnp.abs(positions[None, :] - obs_gcol[:, None])
    distance = jnp.minimum(distance, columns - distance)
    return jnp.maximum(0.0, 1.0 - distance.astype(jnp.float32) / RADIUS)


def vertical(lev_obs, level_arr):
    inverse = 1.0 / (MEMBERS - 1)
    reach_sq = float(VREACH * VREACH)
    offset = (lev_obs[:, None] - level_arr[None, :]).astype(jnp.float32)
    return reach_sq / (reach_sq + offset * offset) * inverse


def spread(values):
    return (values - jnp.mean(values, axis=0, keepdims=True)).astype(jnp.bfloat16)


def weights(priors, observed, inv_factor):
    innovation = observed - priors
    half_step = jnp.dot(innovation, inv_factor.T, precision=lax.Precision.HIGHEST)
    return jnp.dot(half_step, inv_factor, precision=lax.Precision.HIGHEST).astype(jnp.bfloat16)


def level_update(dev_level, prior_dev, obs_weight, horiz_taper, vert_weight):
    covar = lax.dot_general(
        prior_dev, dev_level, (((0,), (0,)), ((), ())), preferred_element_type=jnp.float32
    )
    tapered = (covar * horiz_taper * vert_weight).astype(jnp.bfloat16)
    return jnp.dot(obs_weight, tapered, preferred_element_type=jnp.float32)


def assemble(partial_value):
    return lax.psum(partial_value, ("tile", "lev"))


def per_device(ensemble, perturbed, factor, obs_tile, obs_column, obs_level):
    n_tiles = lax.axis_size("tile")
    tile_index = lax.axis_index("tile")
    lev_index = lax.axis_index("lev")
    members, lev_count, col_count = ensemble.shape
    columns = col_count * n_tiles
    batches, obs_count = obs_tile.shape
    current = ensemble.astype(jnp.float32)
    obs_gcol = obs_tile * col_count + obs_column
    positions = tile_index * col_count + lax.iota(jnp.int32, col_count)
    first_level = lev_index * lev_count
    for batch in range(batches):
        owner_lev = obs_level[batch]
        owned = (obs_tile[batch] == tile_index) & (owner_lev // lev_count == lev_index)
        local_index = (
            jnp.clip(owner_lev - first_level, 0, lev_count - 1) * col_count + obs_column[batch]
        )
        picked = jnp.take(current.reshape(members, lev_count * col_count), local_index, axis=1)
        priors = assemble(jnp.where(owned[None, :], picked, 0.0))
        prior_dev = spread(priors)
        obs_weight = weights(priors, perturbed[batch], factor[batch])
        horiz_taper = horizontal(obs_gcol[batch], positions, columns)
        regress_state_dev = spread(current)
        state_dev = regress_state_dev
        lev_obs = obs_level[batch]

        def one_level(level, accumulated):
            dev_level = lax.dynamic_index_in_dim(state_dev, level, 1, keepdims=False)
            vert_weight = vertical(lev_obs, jnp.reshape(first_level + level, (1,)))
            update = level_update(dev_level, prior_dev, obs_weight, horiz_taper, vert_weight)
            return lax.dynamic_update_index_in_dim(accumulated, update, level, 1)

        current = current + lax.fori_loop(
            0, lev_count, one_level, jnp.zeros(state_dev.shape, jnp.float32)
        )
    return current.astype(jnp.bfloat16)


def solution(mesh):
    return jax.shard_map(
        per_device,
        mesh=mesh,
        in_specs=(P(None, "lev", "tile"), P(), P(), P(), P(), P()),
        out_specs=P(None, "lev", "tile"),
        check_vma=False,
    )
```

profile of v0, /device:TPU:1, one launch (start us, length us, event | category | flops | bytes accessed | tf_op | source)
XLA Modules:
  0.0 2156.8 jit_solution(18159960824139229856)
XLA Ops:
  6.5 1.6 slice_add_fusion
  8.2 3.1 copy.39
  11.3 2.7 gather_fusion
  29.5 230.8 %all-reduce.9.cloned.1.call-done = f32[80,256]{0,1:T(8,128)} async-done(((f32[80,256]{0,1:T(8,128)}), f32[80,256]{0,1:T(8,128)}) %all-reduce.9.cloned.1.call-update) | async-done | bytes 81936 | tf_op jit(solution)/shard_map/psum | solution.py:43
  265.3 17.5 while.112
  266.6 1.6 fusion.365
  269.5 1.6 fusion.365
  272.5 1.6 fusion.365
  275.4 1.6 fusion.365
  278.3 1.6 fusion.365
  281.2 1.6 fusion.365
  284.1 1.9 fusion.302
  286.1 2.3 copy.42
  288.4 2.7 gather_fusion.1
  292.3 238.2 %all-reduce.11.cloned.1.call-done = f32[80,256]{0,1:T(8,128)} async-done(((f32[80,256]{0,1:T(8,128)}), f32[80,256]{0,1:T(8,128)}) %all-reduce.11.cloned.1.call-update) | async-done | bytes 81936 | tf_op jit(solution)/shard_map/psum | solution.py:43
  535.5 16.0 while.113
  552.7 2.6 fusion.301
  555.4 2.3 copy.45
  557.7 2.7 gather_fusion.2
  561.6 238.2 %all-reduce.13.cloned.1.call-done = f32[80,256]{0,1:T(8,128)} async-done(((f32[80,256]{0,1:T(8,128)}), f32[80,256]{0,1:T(8,128)}) %all-reduce.13.cloned.1.call-update) | async-done | bytes 81936 | tf_op jit(solution)/shard_map/psum | solution.py:43
  802.5 1.5 fusion.272
  805.2 1.5 broadcast.603.clone.2
  806.7 20.1 while.114
  807.9 2.1 fusion.373
  811.3 2.1 fusion.373
  814.6 2.1 fusion.373
  818.0 2.1 fusion.373
  821.4 2.1 fusion.373
  824.7 2.1 fusion.373
  826.8 3.3 fusion.300
  830.1 3.5 copy.48
  833.6 2.7 gather_fusion.3
  837.7 238.0 %all-reduce.15.cloned.1.call-done = f32[80,256]{0,1:T(8,128)} async-done(((f32[80,256]{0,1:T(8,128)}), f32[80,256]{0,1:T(8,128)}) %all-reduce.15.cloned.1.call-update) | async-done | bytes 81936 | tf_op jit(solution)/shard_map/psum | solution.py:43
  1081.1 1.5 broadcast.603.clone.3
  1082.7 20.3 while.115
  1083.9 2.1 fusion.377
  1087.3 2.1 fusion.377
  1090.7 2.1 fusion.377
  1094.0 2.1 fusion.377
  1097.4 2.1 fusion.377
  1100.8 2.1 fusion.377
  1102.9 3.3 fusion.299
  1106.2 3.5 copy.51
  1109.7 2.7 gather_fusion.4
  1113.7 238.3 %all-reduce.17.cloned.1.call-done = f32[80,256]{0,1:T(8,128)} async-done(((f32[80,256]{0,1:T(8,128)}), f32[80,256]{0,1:T(8,128)}) %all-reduce.17.cloned.1.call-update) | async-done | bytes 81936 | tf_op jit(solution)/shard_map/psum | solution.py:43
  1357.4 1.5 broadcast.603.clone.4
  1358.9 8.7 while.116
  1367.7 3.3 fusion.298
  1371.0 3.5 copy.54
  1374.4 2.7 gather_fusion.5
  1378.4 238.1 %all-reduce.19.cloned.1.call-done = f32[80,256]{0,1:T(8,128)} async-done(((f32[80,256]{0,1:T(8,128)}), f32[80,256]{0,1:T(8,128)}) %all-reduce.19.cloned.1.call-update) | async-done | bytes 81936 | tf_op jit(solution)/shard_map/psum | solution.py:43
  1621.5 4.5 while.117
  1627.3 2.6 fusion.297
  1630.0 2.3 copy.57
  1632.3 2.7 gather_fusion.6
  1636.4 237.9 %all-reduce.21.cloned.1.call-done = f32[80,256]{0,1:T(8,128)} async-done(((f32[80,256]{0,1:T(8,128)}), f32[80,256]{0,1:T(8,128)}) %all-reduce.21.cloned.1.call-update) | async-done | bytes 81936 | tf_op jit(solution)/shard_map/psum | solution.py:43
  1879.3 4.5 while.118
  1885.1 2.6 fusion.296
  1887.8 2.3 copy.60
  1890.1 2.7 gather_fusion.7
  1893.9 238.2 %all-reduce.23.cloned.1.call-done = f32[80,256]{0,1:T(8,128)} async-done(((f32[80,256]{0,1:T(8,128)}), f32[80,256]{0,1:T(8,128)}) %all-reduce.23.cloned.1.call-update) | async-done | bytes 81936 | tf_op jit(solution)/shard_map/psum | solution.py:43
  2136.9 1.5 broadcast.603
  2138.4 8.7 while.119
  2147.2 2.8 add_convert_fusion
  (288 shorter events, 132.4 us)
Async XLA Ops:
  6.5 253.8 %all-reduce.9.cloned.1.call-start = ((), (), s32[]{:S(2)}) async-start(), calls=%async_computation | async-start | bytes 262144 | tf_op jit(solution)/shard_map/psum | solution.py:43
  8.2 5.8 copy-start.11
  8.2 5.8 copy-start.20
  8.2 7.3 copy-start.19
  8.2 8.0 copy-start.5
  11.3 8.9 copy-start.10
  15.5 514.9 %all-reduce.11.cloned.1.call-start = ((), (), s32[]{:S(2)}) async-start(), calls=%async_computation.1 | async-start | bytes 262144 | tf_op jit(solution)/shard_map/psum | solution.py:43
  282.9 1.3 copy-start.6
  286.0 6.0 copy-start.4
  286.0 5.1 copy-start.28
  286.1 5.1 copy-start.39
  291.9 507.8 %all-reduce.13.cloned.1.call-start = ((), (), s32[]{:S(2)}) async-start(), calls=%async_computation.2 | async-start | bytes 262144 | tf_op jit(solution)/shard_map/psum | solution.py:43
  551.5 1.3 copy-start.7
  555.4 5.1 copy-start.27
  555.4 5.1 copy-start.38
  561.2 514.5 %all-reduce.15.cloned.1.call-start = ((), (), s32[]{:S(2)}) async-start(), calls=%async_computation.3 | async-start | bytes 262144 | tf_op jit(solution)/shard_map/psum | solution.py:43
  802.5 4.2 copy-start.12
  830.1 6.2 copy-start.26
  830.1 6.2 copy-start.37
  830.1 7.3 copy-start.1
  837.2 514.8 %all-reduce.17.cloned.1.call-start = ((), (), s32[]{:S(2)}) async-start(), calls=%async_computation.4 | async-start | bytes 262144 | tf_op jit(solution)/shard_map/psum | solution.py:43
  1078.5 4.2 copy-start.13
  1106.2 6.2 copy-start.25
  1106.2 6.2 copy-start.36
  1106.2 7.1 copy-start.2
  1113.3 503.2 %all-reduce.19.cloned.1.call-start = ((), (), s32[]{:S(2)}) async-start(), calls=%async_computation.5 | async-start | bytes 262144 | tf_op jit(solution)/shard_map/psum | solution.py:43
  1113.6 245.3 %copy-start.16 = (s32[1,256]{1,0:T(1,128)S(1)}, s32[1,256]{1,0:T(1,128)}, u32[]{:S(2)}) copy-start(s32[1,256]{1,0:T(1,128)} %get-tuple-element.2209) | copy-start | bytes 3076
  1113.7 245.2 %copy-start.21 = (s32[1024]{0:T(1024)S(1)}, s32[1024]{0:T(1024)}, u32[]{:S(2)}) copy-start(s32[1024]{0:T(1024)} %get-tuple-element.2359) | copy-start | bytes 12292
  1113.7 245.2 %copy-start.32 = (s32[1,256]{1,0:T(1,128)S(1)}, s32[1,256]{1,0:T(1,128)}, u32[]{:S(2)}) copy-start(s32[1,256]{1,0:T(1,128)} %get-tuple-element.1631) | copy-start | bytes 3076
  1354.8 4.2 copy-start.14
  1371.0 6.2 copy-start.24
  1371.0 6.2 copy-start.35
  1371.0 7.1 copy-start.3
  1378.0 496.3 %all-reduce.21.cloned.1.call-start = ((), (), s32[]{:S(2)}) async-start(), calls=%async_computation.6 | async-start | bytes 262144 | tf_op jit(solution)/shard_map/psum | solution.py:43
  1378.4 243.1 %copy-start.18 = (s32[1,256]{1,0:T(1,128)S(1)}, s32[1,256]{1,0:T(1,128)}, u32[]{:S(2)}) copy-start(s32[1,256]{1,0:T(1,128)} %get-tuple-element.2239) | copy-start | bytes 3076
  1378.4 243.1 %copy-start.31 = (s32[1,256]{1,0:T(1,128)S(1)}, s32[1,256]{1,0:T(1,128)}, u32[]{:S(2)}) copy-start(s32[1,256]{1,0:T(1,128)} %get-tuple-element.1630) | copy-start | bytes 3076
  1626.0 1.3 copy-start.8
  1629.9 6.2 copy-start
  1629.9 5.1 copy-start.23
  1630.0 5.1 copy-start.34
  1635.8 496.3 %all-reduce.23.cloned.1.call-start = ((), (), s32[]{:S(2)}) async-start(), calls=%async_computation.7 | async-start | bytes 262144 | tf_op jit(solution)/shard_map/psum | solution.py:43
  1636.4 242.9 %copy-start.15 = (s32[1,256]{1,0:T(1,128)S(1)}, s32[1,256]{1,0:T(1,128)}, u32[]{:S(2)}) copy-start(s32[1,256]{1,0:T(1,128)} %get-tuple-element.2269) | copy-start | bytes 3076
  1636.4 242.9 %copy-start.30 = (s32[1,256]{1,0:T(1,128)S(1)}, s32[1,256]{1,0:T(1,128)}, u32[]{:S(2)}) copy-start(s32[1,256]{1,0:T(1,128)} %get-tuple-element.1629) | copy-start | bytes 3076
  1883.9 1.3 copy-start.9
  1887.7 5.1 copy-start.22
  1887.8 5.1 copy-start.33
  1893.9 244.5 %copy-start.17 = (s32[1,256]{1,0:T(1,128)S(1)}, s32[1,256]{1,0:T(1,128)}, u32[]{:S(2)}) copy-start(s32[1,256]{1,0:T(1,128)} %get-tuple-element.2299) | copy-start | bytes 3076
  1893.9 244.5 %copy-start.29 = (s32[1,256]{1,0:T(1,128)S(1)}, s32[1,256]{1,0:T(1,128)}, u32[]{:S(2)}) copy-start(s32[1,256]{1,0:T(1,128)} %get-tuple-element.1628) | copy-start | bytes 3076
Sparse Core Ops, SparseCore 0:
  15.6 244.6 all-reduce.8
  292.1 238.3 all-reduce.10
  561.4 238.3 all-reduce.12
  837.3 238.3 all-reduce.14
  1113.4 238.5 all-reduce.16
  1378.1 238.3 all-reduce.18
  1636.0 238.3 all-reduce.20
  1893.8 238.3 all-reduce.22
where the time goes:
time: 2160 us
  waiting for transfers between devices  1900 us (88%)
  matrix products  90.4 us (4%)
  other arithmetic  89.1 us (4%)
  local copies, waits for them, and re-layouts  63.5 us (3%)
    psum x8, waiting for transfers between devices, assemble(): return lax.psum(partial_value, ('tile', 'lev'))  1900 us
    dot_general x48, matrix products, level_update(): return jnp.dot(obs_weight, tapered, preferred_element_type=jnp.float32)  69.3 us
  transfers between devices with their start and end apart: 8, of which 8 were waited for; matrix products, arithmetic and copies ran while one was open for 1% of the time, Pallas kernels for 0%

commit v1 on v0

v1 whole, which is shorter than its diff:
```python
import jax
import jax.numpy as jnp
from jax import lax
from jax.experimental import pallas as pl
from jax.experimental.pallas import tpu as pltpu
from jax.sharding import PartitionSpec as P

MEMBERS = 80
OBS = 256
NB = 8
COLS = 1024
LEV = 6
COLUMNS = 32768
RADIUS = 2560
VREACH = 12

HALF = 80
PIECE = 5
PLANE = 16
DEPTH = 8

F32 = jnp.float32
BF16 = jnp.bfloat16


def down(row):
    return jnp.broadcast_to(row, (128, OBS)).T


def inverse_of(value):
    rough = pl.reciprocal(value, approx=True)
    return rough * (2.0 - value * rough)


def exchange_kernel(ens_h, tile_h, col_h, lev_h, fac_h, *refs):
    (obs_out, ghi_out, glo_out), refs = refs[:3], refs[3:]
    taper_out, refs = refs[:NB - 1], refs[NB - 1:]
    exchange_body((ens_h, tile_h, col_h, lev_h, fac_h), obs_out, ghi_out, glo_out, taper_out, *refs)


def exchange_body(given, obs_out, ghi_out, glo_out, taper_out,
                  ens, tile_r, col_r, lev_r, fac, load, buf, r0, s0, r1, s1, r2, s2, full,
                  send0, recv0, send1, recv1, send2, recv2, send3, recv3, send4, recv4):
    t = lax.axis_index("tile")
    l = lax.axis_index("lev")
    core = t % 2
    z_lo = (t // 2) % 4
    x = t // 8
    y = l // 2
    z_hi = l % 2
    plane = x * 4 + y
    z = z_hi * 4 + z_lo

    def plane_peer(d):
        j = (plane + d) % PLANE
        return j, {"tile": (j // 4) * 8 + z_lo * 2 + core, "lev": (j % 4) * 2 + z_hi}

    def depth_peer(d):
        j = (z + d) % DEPTH
        return j, {"tile": x * 8 + (j % 4) * 2 + core, "lev": y * 2 + j // 4}

    loads = [pltpu.make_async_copy(src, dst, load.at[i])
             for i, (src, dst) in enumerate(zip(given, (ens, tile_r, col_r, lev_r, fac)))]
    for i in (1, 2, 3, 0, 4):
        loads[i].start()

    mate = {"tile": t + 1 - 2 * core, "lev": l}
    peers = [mate] + [plane_peer(d)[1] for d in range(1, PLANE)]
    peers += [depth_peer(d)[1] for d in range(1, DEPTH)]
    barrier = pltpu.get_barrier_semaphore()
    for peer in peers:
        pl.semaphore_signal(barrier, inc=1, device_id=peer, device_id_type=pl.DeviceIdType.MESH)

    for i in range(4):
        loads[i].wait()

    def pick(b, carry):
        owned = tile_r[pl.ds(b, 1), :] == t
        column = jnp.where(owned, col_r[pl.ds(b, 1), :], -1)
        level = lev_r[pl.ds(b, 1), :] - l * LEV
        rows = lax.broadcasted_iota(jnp.int32, (COLS, OBS), 0)
        onehot = jnp.where(rows == column, 1.0, 0.0).astype(BF16)
        got = jnp.dot(ens[...], onehot, preferred_element_type=F32)
        total = jnp.zeros((MEMBERS, OBS), F32)
        for v in range(LEV):
            total = total + jnp.where(level == v, got[v * MEMBERS:(v + 1) * MEMBERS], 0.0)
        for h in range(2):
            for mb in range(10):
                buf[b * 20 + h * 10 + mb] = total[mb * 8:mb * 8 + 8, h * 128:h * 128 + 128]
        return carry
    lax.fori_loop(0, NB, pick, 0, unroll=2)

    pl.semaphore_wait(barrier, len(peers))

    order = list(range(1, PLANE)) + [0]
    pair = {}
    for d in order:
        j, _ = plane_peer(d)
        c = pltpu.make_async_remote_copy(
            src_ref=buf.at[pl.ds((1 - core) * HALF + j * PIECE, PIECE)],
            dst_ref=r0.at[j], send_sem=send0.at[d], recv_sem=recv0.at[d],
            device_id=mate, device_id_type=pl.DeviceIdType.MESH)
        c.start()
        pair[d] = c
    spread_out = {}
    for d in order:
        j, peer = plane_peer(d)
        pair[d].wait_recv()
        s0[j] = buf[pl.ds(core * HALF + j * PIECE, PIECE)] + r0[j]
        if d:
            c = pltpu.make_async_remote_copy(
                src_ref=s0.at[j], dst_ref=r1.at[d], send_sem=send1.at[d], recv_sem=recv1.at[d],
                device_id=peer, device_id_type=pl.DeviceIdType.MESH)
            c.start()
            spread_out[d] = c

    loads[4].wait()

    def gram(b, carry):
        f = fac[b]
        g = lax.dot_general(f, f, (((0,), (0,)), ((), ())), precision=lax.Precision.HIGHEST,
                            preferred_element_type=F32)
        hi = g.astype(BF16)
        ghi_out[b] = hi
        glo_out[b] = (g - hi.astype(F32)).astype(BF16)
        return carry
    lax.fori_loop(0, NB, gram, 0)

    reach_sq = float(VREACH * VREACH)
    inverse = 1.0 / (MEMBERS - 1)

    def tapers_of(b):
        gcol_d = down((tile_r[b:b + 1, :] * COLS + col_r[b:b + 1, :]).astype(F32))
        level_d = down(lev_r[b:b + 1, :].astype(F32))

        def later(b2, carry):
            g2 = (tile_r[pl.ds(b2, 1), :] * COLS + col_r[pl.ds(b2, 1), :]).astype(F32)
            l2 = lev_r[pl.ds(b2, 1), :].astype(F32)
            for h in range(2):
                cut = slice(h * 128, h * 128 + 128)
                dist = jnp.abs(gcol_d - g2[:, cut])
                dist = jnp.minimum(dist, COLUMNS - dist)
                taper = jnp.maximum(0.0, 1.0 - dist * (1.0 / RADIUS))
                off = level_d - l2[:, cut]
                vert = (reach_sq * inverse) * inverse_of(reach_sq + off * off)
                place = pl.multiple_of((b2 - b - 1) * OBS + h * 128, 128)
                taper_out[b][:, pl.ds(place, 128)] = taper * vert
            return carry
        lax.fori_loop(b + 1, NB, later, 0)

    total = s0[plane]
    for d in range(1, PLANE):
        spread_out[d].wait_recv()
        total = total + r1[d]
    s1[...] = total
    along = {}
    for d in range(1, DEPTH):
        _, peer = depth_peer(d)
        c = pltpu.make_async_remote_copy(
            src_ref=s1, dst_ref=r2.at[d], send_sem=send2.at[d], recv_sem=recv2.at[d],
            device_id=peer, device_id_type=pl.DeviceIdType.MESH)
        c.start()
        along[d] = c
    for b in range(3):
        tapers_of(b)
    for d in range(1, DEPTH):
        along[d].wait_recv()
        total = total + r2[d]
    s2[...] = total
    full[pl.ds(core * HALF + plane * PIECE, PIECE)] = total

    gathered = {}
    for d in range(1, PLANE):
        _, peer = plane_peer(d)
        c = pltpu.make_async_remote_copy(
            src_ref=s2, dst_ref=full.at[pl.ds(core * HALF + plane * PIECE, PIECE)],
            send_sem=send3.at[d], recv_sem=recv3.at[d],
            device_id=peer, device_id_type=pl.DeviceIdType.MESH)
        c.start()
        gathered[d] = c
    for b in range(3, NB - 1):
        tapers_of(b)
    passed = {}
    for d in range(PLANE):
        j = (plane - d + PLANE) % PLANE
        if d:
            gathered[d].wait_recv()
        part = full.at[pl.ds(core * HALF + j * PIECE, PIECE)]
        c = pltpu.make_async_remote_copy(
            src_ref=part, dst_ref=part, send_sem=send4.at[d], recv_sem=recv4.at[d],
            device_id=mate, device_id_type=pl.DeviceIdType.MESH)
        c.start()
        passed[d] = c
    for d in range(PLANE):
        passed[d].wait_recv()

    def unpack(cb, carry):
        for mb in range(10):
            obs_out[mb * 8:mb * 8 + 8, pl.ds(pl.multiple_of(cb * 128, 128), 128)] = full[cb * 10 + mb]
        return carry
    lax.fori_loop(0, 16, unpack, 0)

    for d in range(PLANE):
        pair[d].wait_send()
        passed[d].wait_send()
        if d:
            spread_out[d].wait_send()
            gathered[d].wait_send()
        if 0 < d < DEPTH:
            along[d].wait_send()


def exchange(ensemble, obs_tile, obs_column, obs_level, factor):
    vmem = pl.BlockSpec(memory_space=pltpu.VMEM)
    dma = pltpu.SemaphoreType.DMA
    piece = (PIECE, 8, 128)
    return pl.pallas_call(
        exchange_kernel,
        out_shape=(
            jax.ShapeDtypeStruct((MEMBERS, NB * OBS), F32),
            jax.ShapeDtypeStruct((NB, OBS, OBS), BF16),
            jax.ShapeDtypeStruct((NB, OBS, OBS), BF16),
        ) + tuple(jax.ShapeDtypeStruct((OBS, (NB - 1 - b) * OBS), F32) for b in range(NB - 1)),
        in_specs=[pl.BlockSpec(memory_space=pltpu.HBM)] * 5,
        out_specs=(vmem,) * (NB + 2),
        scratch_shapes=[
            pltpu.VMEM((LEV * MEMBERS, COLS), BF16),
            pltpu.VMEM((NB, OBS), jnp.int32),
            pltpu.VMEM((NB, OBS), jnp.int32),
            pltpu.VMEM((NB, OBS), jnp.int32),
            pltpu.VMEM((NB, OBS, OBS), F32),
            dma((5,)),
            pltpu.VMEM((2 * HALF, 8, 128), F32),
            pltpu.VMEM((PLANE,) + piece, F32),
            pltpu.VMEM((PLANE,) + piece, F32),
            pltpu.VMEM((PLANE,) + piece, F32),
            pltpu.VMEM(piece, F32),
            pltpu.VMEM((DEPTH,) + piece, F32),
            pltpu.VMEM(piece, F32),
            pltpu.VMEM((2 * HALF, 8, 128), F32),
            dma((PLANE,)), dma((PLANE,)), dma((PLANE,)), dma((PLANE,)),
            dma((DEPTH,)), dma((DEPTH,)),
            dma((PLANE,)), dma((PLANE,)), dma((PLANE,)), dma((PLANE,)),
        ],
        compiler_params=pltpu.CompilerParams(
            collective_id=0, has_side_effects=True, vmem_limit_bytes=14 * 1024 * 1024),
        name="exchange",
    )(ensemble, obs_tile, obs_column, obs_level, factor)


def centred(values):
    return values - jnp.sum(values, axis=0, keepdims=True) * (1.0 / MEMBERS)


def update_kernel(x_ref, obs_ref, pert, ghi, glo, tile_r, col_r, lev_r, *refs):
    tapers, (out, state, aug, horiz) = refs[:NB - 1], refs[NB - 1:]
    t = lax.axis_index("tile")
    first = lax.axis_index("lev") * LEV
    state[...] = x_ref[...].astype(F32)
    aug[...] = obs_ref[...]
    reach_sq = float(VREACH * VREACH)
    inverse = 1.0 / (MEMBERS - 1)
    lanes = lax.broadcasted_iota(jnp.int32, (OBS, 128), 1)

    for b in range(NB):
        priors = aug[:, b * OBS:(b + 1) * OBS]
        prior_dev = centred(priors)
        innovation = pert[b] - priors
        in_hi = innovation.astype(BF16)
        in_lo = (innovation - in_hi.astype(F32)).astype(BF16)
        g_hi = ghi[b]
        weight = (jnp.dot(in_hi, g_hi, preferred_element_type=F32)
                  + jnp.dot(in_lo, g_hi, preferred_element_type=F32)
                  + jnp.dot(in_hi, glo[b], preferred_element_type=F32)).astype(BF16)
        dev_t = prior_dev.T
        if b + 1 < NB:
            rest = slice((b + 1) * OBS, NB * OBS)
            values = aug[:, rest]
            covar = jnp.dot(dev_t.astype(BF16), centred(values).astype(BF16), preferred_element_type=F32)
            tapered = (covar * tapers[b][...]).astype(BF16)
            aug[:, rest] = values + jnp.dot(weight, tapered, preferred_element_type=F32)

        gcol_d = down((tile_r[b:b + 1, :] * COLS + col_r[b:b + 1, :]).astype(F32))
        level_d = down(lev_r[b:b + 1, :].astype(F32))
        for q in range(COLS // 128):
            dist = jnp.abs(gcol_d - (t * COLS + q * 128 + lanes).astype(F32))
            dist = jnp.minimum(dist, COLUMNS - dist)
            horiz[b % 2, :, q * 128:q * 128 + 128] = jnp.maximum(0.0, 1.0 - dist * (1.0 / RADIUS))

        def first_dot(v):
            off = level_d[:, 0:MEMBERS] - (first + v).astype(F32)
            vert = (reach_sq * inverse) / (reach_sq + off * off)
            dev_v = (dev_t * vert).astype(BF16)
            values = state[v * MEMBERS:(v + 1) * MEMBERS, :]
            return jnp.dot(dev_v, centred(values).astype(BF16), preferred_element_type=F32)

        ahead = first_dot(0)
        for v in range(LEV):
            covar = ahead
            if v + 1 < LEV:
                ahead = first_dot(v + 1)
            rows = slice(v * MEMBERS, (v + 1) * MEMBERS)
            tapered = (covar * horiz[b % 2]).astype(BF16)
            values = state[rows, :] + jnp.dot(weight, tapered, preferred_element_type=F32)
            if b + 1 < NB:
                state[rows, :] = values
            else:
                out[rows, :] = values.astype(BF16)


def update(x, obs, perturbed, ghi, glo, obs_tile, obs_column, obs_level, tapers):
    vmem = pl.BlockSpec(memory_space=pltpu.VMEM)
    return pl.pallas_call(
        update_kernel,
        out_shape=jax.ShapeDtypeStruct((LEV * MEMBERS, COLS), BF16),
        in_specs=[vmem] * (8 + NB - 1),
        out_specs=vmem,
        scratch_shapes=[
            pltpu.VMEM((LEV * MEMBERS, COLS), F32),
            pltpu.VMEM((MEMBERS, NB * OBS), F32),
            pltpu.VMEM((2, OBS, COLS), F32),
        ],
        compiler_params=pltpu.CompilerParams(vmem_limit_bytes=28 * 1024 * 1024),
        name="update",
    )(x, obs, perturbed, ghi, glo, obs_tile, obs_column, obs_level, *tapers)


def per_device(ensemble, perturbed, factor, obs_tile, obs_column, obs_level):
    x = ensemble.transpose(1, 0, 2).reshape(LEV * MEMBERS, COLS)
    obs, ghi, glo, *tapers = exchange(x, obs_tile, obs_column, obs_level, factor)
    posterior = update(x, obs, perturbed, ghi, glo, obs_tile, obs_column, obs_level, tapers)
    return posterior.reshape(LEV, MEMBERS, COLS).transpose(1, 0, 2)


def solution(mesh):
    return jax.shard_map(
        per_device,
        mesh=mesh,
        in_specs=(P(None, "lev", "tile"), P(), P(), P(), P(), P()),
        out_specs=P(None, "lev", "tile"),
        check_vma=False,
    )
```

time: 2160 us -> 58.5 us (0.03)
  waiting for transfers between devices: 1900 us -> 0 us
  matrix products: 90.4 us -> 0 us
  other arithmetic: 89.1 us -> 0 us
  local copies, waits for them, and re-layouts: 63.5 us -> 4.9 us
  Pallas kernels: 0 us -> 53.2 us
    psum x8 -> x0, waiting for transfers between devices: 1900 us -> none  [assemble(): return lax.psum(partial_value, ('tile', 'lev'))]
    dot_general x64 -> x0, matrix products: 90.4 us -> none  [the longest x48 69.3 us: level_update(): return jnp.dot(obs_weight, tapered, preferred_element_type=jnp.float32)]
    pallas_call x0 -> x2, Pallas kernels: none -> 53.2 us  [the longest x1 36.4 us: exchange(): pl.pallas_call(exchange_kernel, out_shape=(jax.ShapeDtypeStruct((MEMBERS,...]
    mul x48 -> x0, other arithmetic: 30.3 us -> none  [vertical(): return reach_sq / (reach_sq + offset * offset) * inverse]
    reduce_sum x16 -> x0, other arithmetic: 27.8 us -> none  [spread(): jnp.mean(values, axis=0, keepdims=True)]
    gather x8 -> x0, local copies, waits for them, and re-layouts: 21.9 us -> none  [per_device(): jnp.take(current.reshape(members, lev_count * col_count), local_index, ax...]
  transfers between devices with their start and end apart: 8 -> 0, of which waited for: 8 -> 0; matrix products, arithmetic and copies ran while one was open for 1% -> 0% of each run, Pallas kernels for 0% -> 0%
where the time goes in v1:
time: 58.5 us; the launch traced here: 58.2 us
  Pallas kernels  53.2 us (91%)
  local copies, waits for them, and re-layouts  4.9 us (8%)
    pallas_call x1, Pallas kernels, exchange(): pl.pallas_call(exchange_kernel, out_shape=(jax.ShapeDtypeStruct((MEMBERS,...  36.4 us
    pallas_call x1, Pallas kernels, update(): pl.pallas_call(update_kernel, out_shape=jax.ShapeDtypeStruct((LEV * MEMBE...  16.8 us
    unnamed x20, local copies, waits for them, and re-layouts  4.9 us

profile of v1, /device:TPU:1, one launch (start us, length us, event | category | flops | bytes accessed | tf_op | source)
XLA Modules:
  0.0 58.2 jit_solution(18161636935027743524)
XLA Ops:
  0.0 0.0 copy-start
  0.0 1.2 %copy-done = bf16[80,6,1024]{2,0,1:T(8,128)(2,1)S(1)} copy-done((bf16[80,6,1024]{2,0,1:T(8,128)(2,1)S(1)}, bf16[80,6,1024]{2,0,1:T(8,128)(2,1)}, u32[]{:S(2)}) %copy-start) | copy-done | bytes 983064
  1.2 0.0 copy-start.2
  1.2 1.6 %copy-done.2 = f32[8,256,256]{2,1,0:T(8,128)S(1)} copy-done((f32[8,256,256]{2,1,0:T(8,128)S(1)}, f32[8,256,256]{2,1,0:T(8,128)}, u32[]{:S(2)}) %copy-start.2) | copy-done | bytes 2097176
  2.8 0.0 copy-start.4
  2.8 0.7 %copy-done.4 = s32[8,256]{1,0:T(8,128)S(1)} copy-done((s32[8,256]{1,0:T(8,128)S(1)}, s32[8,256]{1,0:T(8,128)}, u32[]{:S(2)}) %copy-start.4) | copy-done | bytes 8216
  3.5 0.0 copy-start.6
  3.5 0.7 %copy-done.6 = s32[8,256]{1,0:T(8,128)S(1)} copy-done((s32[8,256]{1,0:T(8,128)S(1)}, s32[8,256]{1,0:T(8,128)}, u32[]{:S(2)}) %copy-start.6) | copy-done | bytes 8216
  4.2 0.0 copy-start.8
  4.2 0.7 %copy-done.8 = s32[8,256]{1,0:T(8,128)S(1)} copy-done((s32[8,256]{1,0:T(8,128)S(1)}, s32[8,256]{1,0:T(8,128)}, u32[]{:S(2)}) %copy-start.8) | copy-done | bytes 8216
  4.9 0.0 copy-start.1
  4.9 0.0 copy-start.3
  4.9 0.0 copy-start.5
  4.9 0.0 copy-start.7
  4.9 0.0 copy-start.9
  4.9 36.4 %exchange.1 = (f32[80,2048]{1,0:T(8,128)S(1)}, bf16[8,256,256]{2,1,0:T(8,128)(2,1)S(1)}, bf16[8,256,256]{2,1,0:T(8,128)(2,1)S(1)}, f32[256,1792]{1,0:T(8,128)S(1...) custom-call(bf16[480,1024]{1,0:T(8,128)(2,1)S(1)} %bitcast.6, ...), custom_call_target="tpu_custom_call" | custom-call | tf_op jit(solution)/shard_map/exchange/pallas_call | solution.py:217
  41.3 0.0 copy-done.1
  41.3 0.0 copy-done.3
  41.3 0.0 copy-done.5
  41.3 0.0 copy-done.7
  41.4 0.0 copy-done.9
  41.4 16.8 %update.1 = bf16[480,1024]{1,0:T(8,128)(2,1)} custom-call(bf16[480,1024]{1,0:T(8,128)(2,1)S(1)} %bitcast.7, f32[80,2048]{1,0:T(8,128)S(1)} %get-tuple-element.15.obs_ref, f32[8,80,256]{2,1,0:T(8,128)S(1)} %copy-done.3, bf16[8,256,256]{2,1,0:T(8,128)(2,1)S(1)} %get-tuple-element.16.ghi, bf16[8,256,256]{2,1,0:T(8,128)(2,1)S(1)} %get-tuple-element.17.glo, ...), custom_call_target="tpu_custom_call" | custom-call | tf_op jit(solution)/shard_map/update/pallas_call | solution.py:313
Async XLA Ops:
  0.0 1.2 %copy-start = (bf16[80,6,1024]{2,0,1:T(8,128)(2,1)S(1)}, bf16[80,6,1024]{2,0,1:T(8,128)(2,1)}, u32[]{:S(2)}) copy-start(bf16[80,6,1024]{2,0,1:T(8,128)(2,1)} %param.6) | copy-start | bytes 2949124
  1.2 1.6 %copy-start.2 = (f32[8,256,256]{2,1,0:T(8,128)S(1)}, f32[8,256,256]{2,1,0:T(8,128)}, u32[]{:S(2)}) copy-start(f32[8,256,256]{2,1,0:T(8,128)} %fac_h.1) | copy-start | bytes 6291460
  2.8 0.7 %copy-start.4 = (s32[8,256]{1,0:T(8,128)S(1)}, s32[8,256]{1,0:T(8,128)}, u32[]{:S(2)}) copy-start(s32[8,256]{1,0:T(8,128)} %tile_r.1) | copy-start | bytes 24580
  3.5 0.7 %copy-start.6 = (s32[8,256]{1,0:T(8,128)S(1)}, s32[8,256]{1,0:T(8,128)}, u32[]{:S(2)}) copy-start(s32[8,256]{1,0:T(8,128)} %col_r.1) | copy-start | bytes 24580
  4.2 0.7 %copy-start.8 = (s32[8,256]{1,0:T(8,128)S(1)}, s32[8,256]{1,0:T(8,128)}, u32[]{:S(2)}) copy-start(s32[8,256]{1,0:T(8,128)} %lev_r.1) | copy-start | bytes 24580
  4.9 36.4 %copy-start.1 = (bf16[80,6,1024]{2,0,1:T(8,128)(2,1)S(1)}, bf16[80,6,1024]{2,0,1:T(8,128)(2,1)}, u32[]{:S(2)}) copy-start(bf16[80,6,1024]{2,0,1:T(8,128)(2,1)} %param.6) | copy-start | bytes 2949124
  4.9 36.4 %copy-start.3 = (f32[8,80,256]{2,1,0:T(8,128)S(1)}, f32[8,80,256]{2,1,0:T(8,128)}, u32[]{:S(2)}) copy-start(f32[8,80,256]{2,1,0:T(8,128)} %pert.1) | copy-start | bytes 1966084
  4.9 36.4 %copy-start.5 = (s32[8,256]{1,0:T(8,128)S(1)}, s32[8,256]{1,0:T(8,128)}, u32[]{:S(2)}) copy-start(s32[8,256]{1,0:T(8,128)} %tile_r.1) | copy-start | bytes 24580
  4.9 36.4 %copy-start.7 = (s32[8,256]{1,0:T(8,128)S(1)}, s32[8,256]{1,0:T(8,128)}, u32[]{:S(2)}) copy-start(s32[8,256]{1,0:T(8,128)} %col_r.1) | copy-start | bytes 24580
  4.9 36.5 %copy-start.9 = (s32[8,256]{1,0:T(8,128)S(1)}, s32[8,256]{1,0:T(8,128)}, u32[]{:S(2)}) copy-start(s32[8,256]{1,0:T(8,128)} %lev_r.1) | copy-start | bytes 24580

commit v2 on v1

--- a/solution.py
+++ b/solution.py
@@ -13,6 +13,8 @@
 COLUMNS = 32768
 RADIUS = 2560
 VREACH = 12
+TILES = 32
+NEAR = -(-RADIUS // COLS)
 
 HALF = 80
 PIECE = 5
@@ -88,24 +90,27 @@
             for mb in range(10):
                 buf[b * 20 + h * 10 + mb] = total[mb * 8:mb * 8 + 8, h * 128:h * 128 + 128]
         return carry
-    lax.fori_loop(0, NB, pick, 0, unroll=2)
-
-    pl.semaphore_wait(barrier, len(peers))
+
+    def pair_copy(j):
+        return pltpu.make_async_remote_copy(
+            src_ref=buf.at[pl.ds((1 - core) * HALF + j * PIECE, PIECE)],
+            dst_ref=r0.at[j], send_sem=send0.at[j], recv_sem=recv0.at[j],
+            device_id=mate, device_id_type=pl.DeviceIdType.MESH)
+
+    for step in range(4):
+        from_batch = (step * 2 + 4 * (1 - core)) % NB
+        lax.fori_loop(0, 2, lambda i, c, from_batch=from_batch: pick(from_batch + i, c), 0, unroll=True)
+        if step == 0:
+            pl.semaphore_wait(barrier, len(peers))
+        if step < 2:
+            for j in range(step * 8, step * 8 + 8):
+                pair_copy(j).start()
 
     order = list(range(1, PLANE)) + [0]
-    pair = {}
-    for d in order:
-        j, _ = plane_peer(d)
-        c = pltpu.make_async_remote_copy(
-            src_ref=buf.at[pl.ds((1 - core) * HALF + j * PIECE, PIECE)],
-            dst_ref=r0.at[j], send_sem=send0.at[d], recv_sem=recv0.at[d],
-            device_id=mate, device_id_type=pl.DeviceIdType.MESH)
-        c.start()
-        pair[d] = c
     spread_out = {}
     for d in order:
         j, peer = plane_peer(d)
-        pair[d].wait_recv()
+        pair_copy(j).wait_recv()
         s0[j] = buf[pl.ds(core * HALF + j * PIECE, PIECE)] + r0[j]
         if d:
             c = pltpu.make_async_remote_copy(
@@ -201,7 +206,7 @@
     lax.fori_loop(0, 16, unpack, 0)
 
     for d in range(PLANE):
-        pair[d].wait_send()
+        pair_copy(d).wait_send()
         passed[d].wait_send()
         if d:
             spread_out[d].wait_send()
@@ -245,7 +250,8 @@
         compiler_params=pltpu.CompilerParams(
             collective_id=0, has_side_effects=True, vmem_limit_bytes=14 * 1024 * 1024),
         name="exchange",
-    )(ensemble, obs_tile, obs_column, obs_level, factor)
+    )(*(pltpu.with_memory_space_constraint(a, pltpu.HBM)
+        for a in (ensemble, obs_tile, obs_column, obs_level, factor)))
 
 
 def centred(values):
@@ -253,14 +259,24 @@
 
 
 def update_kernel(x_ref, obs_ref, pert, ghi, glo, tile_r, col_r, lev_r, *refs):
-    tapers, (out, state, aug, horiz) = refs[:NB - 1], refs[NB - 1:]
+    tapers = refs[:NB - 1]
+    out, state, aug, devs, weights, gcols, levels, horiz, counts = refs[NB - 1:]
     t = lax.axis_index("tile")
     first = lax.axis_index("lev") * LEV
     state[...] = x_ref[...].astype(F32)
     aug[...] = obs_ref[...]
     reach_sq = float(VREACH * VREACH)
     inverse = 1.0 / (MEMBERS - 1)
-    lanes = lax.broadcasted_iota(jnp.int32, (OBS, 128), 1)
+
+    low = (t + TILES - NEAR) % TILES
+    turns = []
+    for b in range(NB):
+        owner = tile_r[b:b + 1, :]
+        rel = owner - low
+        rel = jnp.where(rel < 0, rel + TILES, rel)
+        counts[b] = jnp.sum(jnp.where(rel < 2 * NEAR + 1, 1.0, 0.0)).astype(jnp.int32)
+        skipped = jnp.sum(jnp.where(owner < low, 1.0, 0.0)).astype(jnp.int32)
+        turns.append(lax.rem(OBS - skipped, OBS))
 
     for b in range(NB):
         priors = aug[:, b * OBS:(b + 1) * OBS]
@@ -269,30 +285,41 @@
         in_hi = innovation.astype(BF16)
         in_lo = (innovation - in_hi.astype(F32)).astype(BF16)
         g_hi = ghi[b]
-        weight = (jnp.dot(in_hi, g_hi, preferred_element_type=F32)
-                  + jnp.dot(in_lo, g_hi, preferred_element_type=F32)
-                  + jnp.dot(in_hi, glo[b], preferred_element_type=F32)).astype(BF16)
-        dev_t = prior_dev.T
+        full_weight = (jnp.dot(in_hi, g_hi, preferred_element_type=F32)
+                       + jnp.dot(in_lo, g_hi, preferred_element_type=F32)
+                       + jnp.dot(in_hi, glo[b], preferred_element_type=F32))
         if b + 1 < NB:
             rest = slice((b + 1) * OBS, NB * OBS)
             values = aug[:, rest]
-            covar = jnp.dot(dev_t.astype(BF16), centred(values).astype(BF16), preferred_element_type=F32)
+            covar = jnp.dot(prior_dev.T.astype(BF16), centred(values).astype(BF16),
+                            preferred_element_type=F32)
             tapered = (covar * tapers[b][...]).astype(BF16)
-            aug[:, rest] = values + jnp.dot(weight, tapered, preferred_element_type=F32)
-
-        gcol_d = down((tile_r[b:b + 1, :] * COLS + col_r[b:b + 1, :]).astype(F32))
-        level_d = down(lev_r[b:b + 1, :].astype(F32))
+            aug[:, rest] = values + jnp.dot(full_weight.astype(BF16), tapered,
+                                            preferred_element_type=F32)
+        devs[b] = pltpu.roll(prior_dev, turns[b], 1).T
+        weights[b] = pltpu.roll(full_weight, turns[b], 1).astype(BF16)
+        gcol = (tile_r[b:b + 1, :] * COLS + col_r[b:b + 1, :]).astype(F32)
+        gcols[b] = pltpu.roll(jnp.broadcast_to(gcol, (128, OBS)), turns[b], 1).T
+        lev = lev_r[b:b + 1, :].astype(F32)
+        levels[b] = pltpu.roll(jnp.broadcast_to(lev, (128, OBS)), turns[b], 1).T
+
+    def regress(b, width):
+        lanes = lax.broadcasted_iota(jnp.int32, (width, 128), 1)
+        gcol_d = gcols[b, 0:width]
         for q in range(COLS // 128):
             dist = jnp.abs(gcol_d - (t * COLS + q * 128 + lanes).astype(F32))
             dist = jnp.minimum(dist, COLUMNS - dist)
-            horiz[b % 2, :, q * 128:q * 128 + 128] = jnp.maximum(0.0, 1.0 - dist * (1.0 / RADIUS))
+            horiz[0:width, q * 128:q * 128 + 128] = jnp.maximum(0.0, 1.0 - dist * (1.0 / RADIUS))
+        weight = weights[b][:, 0:width]
+        level_d = levels[b, 0:width, 0:MEMBERS]
+        dev_t = devs[b, 0:width, :]
 
         def first_dot(v):
-            off = level_d[:, 0:MEMBERS] - (first + v).astype(F32)
-            vert = (reach_sq * inverse) / (reach_sq + off * off)
-            dev_v = (dev_t * vert).astype(BF16)
+            off = level_d - (first + v).astype(F32)
+            vert = (reach_sq * inverse) * inverse_of(reach_sq + off * off)
             values = state[v * MEMBERS:(v + 1) * MEMBERS, :]
-            return jnp.dot(dev_v, centred(values).astype(BF16), preferred_element_type=F32)
+            return jnp.dot((dev_t * vert).astype(BF16), centred(values).astype(BF16),
+                           preferred_element_type=F32)
 
         ahead = first_dot(0)
         for v in range(LEV):
@@ -300,12 +327,22 @@
             if v + 1 < LEV:
                 ahead = first_dot(v + 1)
             rows = slice(v * MEMBERS, (v + 1) * MEMBERS)
-            tapered = (covar * horiz[b % 2]).astype(BF16)
-            values = state[rows, :] + jnp.dot(weight, tapered, preferred_element_type=F32)
-            if b + 1 < NB:
-                state[rows, :] = values
-            else:
-                out[rows, :] = values.astype(BF16)
+            tapered = (covar * horiz[0:width, :]).astype(BF16)
+            state[rows, :] = state[rows, :] + jnp.dot(weight, tapered, preferred_element_type=F32)
+
+    def batch(b, carry):
+        near = counts[b]
+
+        @pl.when(near <= OBS // 2)
+        def _():
+            regress(b, OBS // 2)
+
+        @pl.when(near > OBS // 2)
+        def _():
+            regress(b, OBS)
+        return carry
+    lax.fori_loop(0, NB, batch, 0)
+    out[...] = state[...].astype(BF16)
 
 
 def update(x, obs, perturbed, ghi, glo, obs_tile, obs_column, obs_level, tapers):
@@ -318,7 +355,12 @@
         scratch_shapes=[
             pltpu.VMEM((LEV * MEMBERS, COLS), F32),
             pltpu.VMEM((MEMBERS, NB * OBS), F32),
-            pltpu.VMEM((2, OBS, COLS), F32),
+            pltpu.VMEM((NB, OBS, MEMBERS), F32),
+            pltpu.VMEM((NB, MEMBERS, OBS), BF16),
+            pltpu.VMEM((NB, OBS, 128), F32),
+            pltpu.VMEM((NB, OBS, 128), F32),
+            pltpu.VMEM((OBS, COLS), F32),
+            pltpu.SMEM((NB,), jnp.int32),
         ],
         compiler_params=pltpu.CompilerParams(vmem_limit_bytes=28 * 1024 * 1024),
         name="update",

time: 58.5 us -> 49.5 us (0.85)
  local copies, waits for them, and re-layouts: 4.9 us -> 0.02 us
  Pallas kernels: 53.2 us -> 49.3 us
    unnamed x20 -> x10, local copies, waits for them, and re-layouts: 4.9 us -> 0.02 us
    pallas_call x1, Pallas kernels: 16.8 us -> 13.9 us  [update(): pl.pallas_call(update_kernel, out_shape=jax.ShapeDtypeStruct((LEV * MEMBE...]
    pallas_call x1, Pallas kernels: 36.4 us -> 35.4 us  [exchange(): pl.pallas_call(exchange_kernel, out_shape=(jax.ShapeDtypeStruct((MEMBERS,...]
where the time goes in v2:
time: 49.5 us; the launch traced here: 49.4 us
  Pallas kernels  49.3 us (100%)
    pallas_call x1, Pallas kernels, exchange(): pl.pallas_call(exchange_kernel, out_shape=(jax.ShapeDtypeStruct((MEMBERS,...  35.4 us
    pallas_call x1, Pallas kernels, update(): pl.pallas_call(update_kernel, out_shape=jax.ShapeDtypeStruct((LEV * MEMBE...  13.9 us

profile of v2, /device:TPU:1, one launch (start us, length us, event | category | flops | bytes accessed | tf_op | source)
XLA Modules:
  0.0 49.4 jit_solution(11213703662739513550)
XLA Ops:
  0.0 0.0 copy-start.4
  0.0 0.0 copy-start.3
  0.0 0.0 copy-start.2
  0.0 0.0 copy-start.1
  0.0 0.0 copy-start
  0.0 35.4 %exchange.1 = (f32[80,2048]{1,0:T(8,128)S(1)}, bf16[8,256,256]{2,1,0:T(8,128)(2,1)S(1)}, bf16[8,256,256]{2,1,0:T(8,128)(2,1)S(1)}, f32[256,1792]{1,0:T(8,128)S(1...) custom-call(bf16[480,1024]{1,0:T(8,128)(2,1)} %bitcast.6, ...), custom_call_target="tpu_custom_call" | custom-call | tf_op jit(solution)/shard_map/exchange/pallas_call | solution.py:222
  35.5 0.0 copy-done.4
  35.5 0.0 copy-done.3
  35.5 0.0 copy-done.2
  35.5 0.0 copy-done.1
  35.5 0.0 copy-done
  35.5 13.9 %update.1 = bf16[480,1024]{1,0:T(8,128)(2,1)} custom-call(bf16[480,1024]{1,0:T(8,128)(2,1)S(1)} %bitcast.7, f32[80,2048]{1,0:T(8,128)S(1)} %get-tuple-element.15.obs_ref, f32[8,80,256]{2,1,0:T(8,128)S(1)} %copy-done.1, bf16[8,256,256]{2,1,0:T(8,128)(2,1)S(1)} %get-tuple-element.16.ghi, bf16[8,256,256]{2,1,0:T(8,128)(2,1)S(1)} %get-tuple-element.17.glo, ...), custom_call_target="tpu_custom_call" | custom-call | tf_op jit(solution)/shard_map/update/pallas_call | solution.py:350
Async XLA Ops:
  0.0 35.5 %copy-start.4 = (s32[8,256]{1,0:T(8,128)S(1)}, s32[8,256]{1,0:T(8,128)}, u32[]{:S(2)}) copy-start(s32[8,256]{1,0:T(8,128)} %lev_r.1) | copy-start | bytes 24580
  0.0 35.5 %copy-start.3 = (s32[8,256]{1,0:T(8,128)S(1)}, s32[8,256]{1,0:T(8,128)}, u32[]{:S(2)}) copy-start(s32[8,256]{1,0:T(8,128)} %col_r.1) | copy-start | bytes 24580
  0.0 35.5 %copy-start.2 = (s32[8,256]{1,0:T(8,128)S(1)}, s32[8,256]{1,0:T(8,128)}, u32[]{:S(2)}) copy-start(s32[8,256]{1,0:T(8,128)} %tile_r.1) | copy-start | bytes 24580
  0.0 35.5 %copy-start.1 = (f32[8,80,256]{2,1,0:T(8,128)S(1)}, f32[8,80,256]{2,1,0:T(8,128)}, u32[]{:S(2)}) copy-start(f32[8,80,256]{2,1,0:T(8,128)} %pert.1) | copy-start | bytes 1966084
  0.0 35.5 %copy-start = (bf16[80,6,1024]{2,0,1:T(8,128)(2,1)S(1)}, bf16[80,6,1024]{2,0,1:T(8,128)(2,1)}, u32[]{:S(2)}) copy-start(bf16[80,6,1024]{2,0,1:T(8,128)(2,1)} %param.6) | copy-start | bytes 2949124
